TPU v7x, 128 devices: a whole 4x4x4 slice. The times are simulated.
128 devices in a mesh: seq: 16 (over x_hi, y, core), grp: 8 (over z, x_lo).
Axes of the slice: x: 4 (x_hi: 2, x_lo: 2; x = x_hi * 2 + x_lo), y: 4, z: 4, core: 2. Of those that a mesh axis runs over, the one named last changes fastest.
Arguments:
- tile_embeds: bfloat16 [1536, 18432], P('grp', 'seq'), may hold values from -6 to 6
- w_in: bfloat16 [1536, 768], P('grp'), may hold values from -0.15625 to 0.15625
- perturb: bfloat16 [1536, 768], P('grp'), may hold values from -0.078125 to 0.078125
- gain_attn: float32 [768], replicated, may hold values from 0.25 to 1.75
- w_qkv: bfloat16 [768, 2304], replicated, may hold values from -0.25 to 0.25
- temper: float32 [12], replicated, may hold values from 1.5 to 16
- w_out: bfloat16 [768, 768], replicated, may hold values from -0.21875 to 0.21875
- gain_mlp: float32 [768], replicated, may hold values from 0.25 to 1.75
- w_up: bfloat16 [768, 3072], replicated, may hold values from -0.21875 to 0.21875
- w_down: bfloat16 [3072, 768], replicated, may hold values from -0.109375 to 0.109375
Outputs:
- encoded: bfloat16 [18432, 768], P(('seq', 'grp'))
All inputs are finite; a program needn't handle non-finite values.
Results may differ from a plain program's by a relative error of at most 0.018.
Values may be sent and summed in bfloat16 or wider, within the bound.
A program may use at most 128 MiB of HBM per device.

v0:
```python
import jax
import jax.numpy as jnp
from jax import lax
from jax.sharding import PartitionSpec as P


def shifted(value, axis, steps):
    count = lax.axis_size(axis)
    pairs = [(source, (source + steps) % count) for source in range(count)]
    return lax.ppermute(value, axis, pairs)


def norm_rows(values, gain):
    floats = values.astype(jnp.float32)
    average = jnp.mean(floats, axis=-1, keepdims=True)
    centred = floats - average
    spread = jnp.mean(centred * centred, axis=-1, keepdims=True)
    return (centred * lax.rsqrt(spread + 1e-05) * gain).astype(jnp.bfloat16)


def contract_first(features, weight):
    return lax.dot_general(
        features, weight, (((0,), (0,)), ((), ())), preferred_element_type=jnp.float32
    )


def on_device(tile_embeds, w_in, perturb, gain_attn, w_qkv, temper, w_out, gain_mlp, w_up, w_down):
    group_count = lax.axis_size("grp")
    seq_count = lax.axis_size("seq")
    block_total = tile_embeds.shape[1]
    row_count = block_total // group_count
    model_width = w_qkv.shape[0]
    head_count = temper.shape[0]
    head_size = model_width // head_count
    w_eff = (w_in.astype(jnp.float32) + perturb.astype(jnp.float32)).astype(jnp.bfloat16)
    embedded = lax.psum_scatter(
        contract_first(tile_embeds, w_eff), "grp", scatter_dimension=0, tiled=True
    )
    hidden = embedded.astype(jnp.bfloat16)
    normed_attn = norm_rows(hidden, gain_attn)
    projected = jnp.dot(normed_attn, w_qkv, preferred_element_type=jnp.float32)
    query = projected[:, :model_width].astype(jnp.bfloat16)
    key_rows = projected[:, model_width : 2 * model_width].astype(jnp.bfloat16)
    value_rows = projected[:, 2 * model_width :].astype(jnp.bfloat16)
    block_queries = lax.all_gather(query, "grp", axis=0, tiled=True).reshape(
        block_total, head_count, head_size
    )
    score_scale = temper * head_size ** (-0.5)

    def absorb(softmax_state, kv_block):
        running_max, running_sum, running_acc = softmax_state
        key_heads = kv_block[0].reshape(row_count, head_count, head_size)
        value_heads = kv_block[1].reshape(row_count, head_count, head_size)
        scores = (
            jnp.einsum("qhd,khd->qhk", block_queries, key_heads, preferred_element_type=jnp.float32)
            * score_scale[None, :, None]
        )
        new_max = jnp.maximum(running_max, jnp.max(scores, axis=-1))
        rescale = jnp.exp(running_max - new_max)
        expo = jnp.exp(scores - new_max[:, :, None])
        new_sum = running_sum * rescale + jnp.sum(expo, axis=-1)
        added = jnp.einsum(
            "qhk,khd->qhd",
            expo.astype(jnp.bfloat16),
            value_heads,
            preferred_element_type=jnp.float32,
        )
        new_acc = running_acc * rescale[:, :, None] + added
        return (new_max, new_sum, new_acc)

    kv_own = jnp.stack([key_rows, value_rows])
    start_state = (
        jnp.full((block_total, head_count), -jnp.inf, jnp.float32),
        jnp.zeros((block_total, head_count), jnp.float32),
        jnp.zeros((block_total, head_count, head_size), jnp.float32),
    )
    softmax_state = absorb(start_state, kv_own)

    def travel(step_index, carried):
        inner_state, moving = carried
        moving = shifted(moving, "seq", 1)
        return (absorb(inner_state, moving), moving)

    softmax_state, kv_last = lax.fori_loop(0, seq_count - 1, travel, (softmax_state, kv_own))
    running_max, running_sum, running_acc = softmax_state
    part_acc, part_max, part_sum = (
        lax.all_to_all(
            running_acc.reshape(1, block_total, model_width),
            "grp",
            split_axis=1,
            concat_axis=0,
            tiled=True,
        ),
        lax.all_to_all(running_max[None], "grp", split_axis=1, concat_axis=0, tiled=True),
        lax.all_to_all(running_sum[None], "grp", split_axis=1, concat_axis=0, tiled=True),
    )
    overall_max = jnp.max(part_max, axis=0)
    factors = jnp.exp(part_max - overall_max[None])
    part_acc = part_acc.reshape(group_count, row_count, head_count, head_size)
    numerator = jnp.sum(part_acc * factors[:, :, :, None], axis=0)
    denominator = jnp.sum(part_sum * factors, axis=0)
    attended = (
        (numerator / denominator[:, :, None]).reshape(row_count, model_width).astype(jnp.bfloat16)
    )
    mixed = jnp.dot(attended, w_out, preferred_element_type=jnp.float32)
    resid = (hidden.astype(jnp.float32) + mixed).astype(jnp.bfloat16)
    normed_mlp = norm_rows(resid, gain_mlp)
    raised = jnp.dot(normed_mlp, w_up, preferred_element_type=jnp.float32)
    activated = jax.nn.gelu(raised).astype(jnp.bfloat16)
    lowered = jnp.dot(activated, w_down, preferred_element_type=jnp.float32)
    return (resid.astype(jnp.float32) + lowered).astype(jnp.bfloat16)


def solution(mesh):
    placed = (P("grp", "seq"), P("grp", None), P("grp", None), P(), P(), P(), P(), P(), P(), P())
    return jax.shard_map(
        on_device, mesh=mesh, in_specs=placed, out_specs=P(("seq", "grp"), None), check_vma=False
    )
```

profile of v0, /device:TPU:0, one launch (start us, length us, event | category | flops | bytes accessed | tf_op | source)
XLA Modules:
  0.0 653.4 jit_solution(15127057999903708839)
XLA Ops:
  6.5 3.9 convolution_bitcast_fusion
  10.4 5.2 copy.54
  15.7 81.9 %reduce-scatter.4.cloned.1.call-done = f32[144,768]{1,0:T(8,128)} async-done(((f32[1152,768]{1,0:T(8,128)}), f32[144,768]{1,0:T(8,128)}) %reduce-scatter.4.cloned.1.call-update) | async-done | bytes 442384 | tf_op jit(solution)/shard_map/reduce_scatter | solution.py:36
  102.4 44.1 %all-gather.2.cloned.1.call-done = bf16[1152,768]{1,0:T(8,128)(2,1)} async-done(((bf16[144,768]{1,0:T(8,128)(2,1)}), bf16[1152,768]{1,0:T(8,128)(2,1)}) %all-gather.2.cloned.1.call-update) | async-done | bytes 1769488 | tf_op jit(solution)/shard_map/all_gather | solution.py:45
  146.5 2.7 copy.42
  154.6 402.8 %while.16 = (s32[]{:T(128)}, f32[1152,12]{0,1:T(8,128)}, f32[1152,12]{0,1:T(8,128)}, f32[1152,12,64]{0,2,1:T(8,128)S(1)}, bf16[2,144,768]{2,1,0:T(8,128)(2,1)}, ...) while((s32[]{:T(128)}, f32[1152,12]{0,1:T(8,128)}, f32[1152,12]{0,1:T(8,128)}, ...), condition=%wide.region_8.0_spmd, body=%wide.region_5.0_spmd.sunk | while | flops 527330304 | bytes 40034684 | solution.py:84
  154.7 11.6 %collective-permute-done = bf16[2,144,768]{2,1,0:T(8,128)(2,1)} collective-permute-done((bf16[2,144,768]{2,1,0:T(8,128)(2,1)}, bf16[2,144,768]{2,1,0:T(8,128)(2,1)}, u32[]{:S(2)}, u32[]{:S(2)}) %collective-permute-start) | collective-permute-done | bytes 442400 | tf_op jit(solution)/shard_map/while/body/eval_jaxpr/ppermute | solution.py:10
  171.9 3.0 bitcast_reduce_fusion.3
  181.6 11.7 %collective-permute-done = bf16[2,144,768]{2,1,0:T(8,128)(2,1)} collective-permute-done((bf16[2,144,768]{2,1,0:T(8,128)(2,1)}, bf16[2,144,768]{2,1,0:T(8,128)(2,1)}, u32[]{:S(2)}, u32[]{:S(2)}) %collective-permute-start) | collective-permute-done | bytes 442400 | tf_op jit(solution)/shard_map/while/body/eval_jaxpr/ppermute | solution.py:10
  198.8 3.0 bitcast_reduce_fusion.3
  204.1 2.5 fusion.89
  208.4 11.7 %collective-permute-done = bf16[2,144,768]{2,1,0:T(8,128)(2,1)} collective-permute-done((bf16[2,144,768]{2,1,0:T(8,128)(2,1)}, bf16[2,144,768]{2,1,0:T(8,128)(2,1)}, u32[]{:S(2)}, u32[]{:S(2)}) %collective-permute-start) | collective-permute-done | bytes 442400 | tf_op jit(solution)/shard_map/while/body/eval_jaxpr/ppermute | solution.py:10
  225.6 3.0 bitcast_reduce_fusion.3
  230.9 2.5 fusion.89
  235.3 11.7 %collective-permute-done = bf16[2,144,768]{2,1,0:T(8,128)(2,1)} collective-permute-done((bf16[2,144,768]{2,1,0:T(8,128)(2,1)}, bf16[2,144,768]{2,1,0:T(8,128)(2,1)}, u32[]{:S(2)}, u32[]{:S(2)}) %collective-permute-start) | collective-permute-done | bytes 442400 | tf_op jit(solution)/shard_map/while/body/eval_jaxpr/ppermute | solution.py:10
  252.5 3.0 bitcast_reduce_fusion.3
  262.1 11.7 %collective-permute-done = bf16[2,144,768]{2,1,0:T(8,128)(2,1)} collective-permute-done((bf16[2,144,768]{2,1,0:T(8,128)(2,1)}, bf16[2,144,768]{2,1,0:T(8,128)(2,1)}, u32[]{:S(2)}, u32[]{:S(2)}) %collective-permute-start) | collective-permute-done | bytes 442400 | tf_op jit(solution)/shard_map/while/body/eval_jaxpr/ppermute | solution.py:10
  279.3 3.0 bitcast_reduce_fusion.3
  289.0 11.7 %collective-permute-done = bf16[2,144,768]{2,1,0:T(8,128)(2,1)} collective-permute-done((bf16[2,144,768]{2,1,0:T(8,128)(2,1)}, bf16[2,144,768]{2,1,0:T(8,128)(2,1)}, u32[]{:S(2)}, u32[]{:S(2)}) %collective-permute-start) | collective-permute-done | bytes 442400 | tf_op jit(solution)/shard_map/while/body/eval_jaxpr/ppermute | solution.py:10
  306.2 3.0 bitcast_reduce_fusion.3
  315.8 11.7 %collective-permute-done = bf16[2,144,768]{2,1,0:T(8,128)(2,1)} collective-permute-done((bf16[2,144,768]{2,1,0:T(8,128)(2,1)}, bf16[2,144,768]{2,1,0:T(8,128)(2,1)}, u32[]{:S(2)}, u32[]{:S(2)}) %collective-permute-start) | collective-permute-done | bytes 442400 | tf_op jit(solution)/shard_map/while/body/eval_jaxpr/ppermute | solution.py:10
  333.0 3.0 bitcast_reduce_fusion.3
  342.6 11.7 %collective-permute-done = bf16[2,144,768]{2,1,0:T(8,128)(2,1)} collective-permute-done((bf16[2,144,768]{2,1,0:T(8,128)(2,1)}, bf16[2,144,768]{2,1,0:T(8,128)(2,1)}, u32[]{:S(2)}, u32[]{:S(2)}) %collective-permute-start) | collective-permute-done | bytes 442400 | tf_op jit(solution)/shard_map/while/body/eval_jaxpr/ppermute | solution.py:10
  359.9 3.0 bitcast_reduce_fusion.3
  369.5 11.7 %collective-permute-done = bf16[2,144,768]{2,1,0:T(8,128)(2,1)} collective-permute-done((bf16[2,144,768]{2,1,0:T(8,128)(2,1)}, bf16[2,144,768]{2,1,0:T(8,128)(2,1)}, u32[]{:S(2)}, u32[]{:S(2)}) %collective-permute-start) | collective-permute-done | bytes 442400 | tf_op jit(solution)/shard_map/while/body/eval_jaxpr/ppermute | solution.py:10
  386.7 3.0 bitcast_reduce_fusion.3
  396.3 11.7 %collective-permute-done = bf16[2,144,768]{2,1,0:T(8,128)(2,1)} collective-permute-done((bf16[2,144,768]{2,1,0:T(8,128)(2,1)}, bf16[2,144,768]{2,1,0:T(8,128)(2,1)}, u32[]{:S(2)}, u32[]{:S(2)}) %collective-permute-start) | collective-permute-done | bytes 442400 | tf_op jit(solution)/shard_map/while/body/eval_jaxpr/ppermute | solution.py:10
  413.5 3.0 bitcast_reduce_fusion.3
  423.2 11.7 %collective-permute-done = bf16[2,144,768]{2,1,0:T(8,128)(2,1)} collective-permute-done((bf16[2,144,768]{2,1,0:T(8,128)(2,1)}, bf16[2,144,768]{2,1,0:T(8,128)(2,1)}, u32[]{:S(2)}, u32[]{:S(2)}) %collective-permute-start) | collective-permute-done | bytes 442400 | tf_op jit(solution)/shard_map/while/body/eval_jaxpr/ppermute | solution.py:10
  440.4 3.0 bitcast_reduce_fusion.3
  450.0 11.7 %collective-permute-done = bf16[2,144,768]{2,1,0:T(8,128)(2,1)} collective-permute-done((bf16[2,144,768]{2,1,0:T(8,128)(2,1)}, bf16[2,144,768]{2,1,0:T(8,128)(2,1)}, u32[]{:S(2)}, u32[]{:S(2)}) %collective-permute-start) | collective-permute-done | bytes 442400 | tf_op jit(solution)/shard_map/while/body/eval_jaxpr/ppermute | solution.py:10
  467.2 3.0 bitcast_reduce_fusion.3
  476.9 11.7 %collective-permute-done = bf16[2,144,768]{2,1,0:T(8,128)(2,1)} collective-permute-done((bf16[2,144,768]{2,1,0:T(8,128)(2,1)}, bf16[2,144,768]{2,1,0:T(8,128)(2,1)}, u32[]{:S(2)}, u32[]{:S(2)}) %collective-permute-start) | collective-permute-done | bytes 442400 | tf_op jit(solution)/shard_map/while/body/eval_jaxpr/ppermute | solution.py:10
  494.1 3.0 bitcast_reduce_fusion.3
  503.7 11.7 %collective-permute-done = bf16[2,144,768]{2,1,0:T(8,128)(2,1)} collective-permute-done((bf16[2,144,768]{2,1,0:T(8,128)(2,1)}, bf16[2,144,768]{2,1,0:T(8,128)(2,1)}, u32[]{:S(2)}, u32[]{:S(2)}) %collective-permute-start) | collective-permute-done | bytes 442400 | tf_op jit(solution)/shard_map/while/body/eval_jaxpr/ppermute | solution.py:10
  520.9 3.0 bitcast_reduce_fusion.3
  530.6 11.7 %collective-permute-done = bf16[2,144,768]{2,1,0:T(8,128)(2,1)} collective-permute-done((bf16[2,144,768]{2,1,0:T(8,128)(2,1)}, bf16[2,144,768]{2,1,0:T(8,128)(2,1)}, u32[]{:S(2)}, u32[]{:S(2)}) %collective-permute-start) | collective-permute-done | bytes 442400 | tf_op jit(solution)/shard_map/while/body/eval_jaxpr/ppermute | solution.py:10
  547.8 3.0 bitcast_reduce_fusion.3
  559.9 7.5 %reduce.3 = f32[1152,12]{1,0:T(8,128)} reduce(f32[1152,1,12]{2,1,0:T(1,128)} %bitcast.99, f32[]{:T(128)} %broadcast.83), dimensions={1}, to_apply=%bitcast.56.reduce_sub_computation | reduce | bytes 110596
  569.5 4.0 all-to-all-start.1
  575.4 7.3 %reduce.1 = f32[1152,12]{1,0:T(8,128)} reduce(f32[1152,1,12]{2,1,0:T(1,128)} %bitcast.100, f32[]{:T(128)} %broadcast.83), dimensions={1}, to_apply=%bitcast.58.reduce_sub_computation | reduce | bytes 110596
  584.8 5.6 all-to-all-start.2
  590.4 6.1 copy.44
  596.9 7.3 %all-to-all-start = ((f32[1,1152,768]{2,0,1:T(1,128)}), f32[1,1152,768]{2,0,1:T(1,128)}, u32[]{:S(2)}, u32[]{:S(2)}) async-start(f32[1,1152,768]{2,0,1:T(1,128)} %copy.44), calls=%async_computation | async-start | bytes 7077888 | tf_op jit(solution)/shard_map/all_to_all | solution.py:87
  610.2 3.2 mul.136
  613.3 4.3 copy.48
  620.7 14.0 %all-to-all-done = f32[1,1152,768]{2,0,1:T(1,128)} async-done(((f32[1,1152,768]{2,0,1:T(1,128)}), f32[1,1152,768]{2,0,1:T(1,128)}, u32[]{:S(2)}, u32[]{:S(2)}) %all-to-all-start) | async-done | bytes 3538976 | tf_op jit(solution)/shard_map/all_to_all | solution.py:87
  639.9 6.7 %fusion.36 = bf16[144,768]{1,0:T(8,128)(2,1)} fusion(f32[144,768]{1,0:T(8,128)} %copy-done.12, bf16[3072,768]{1,0:T(8,128)(2,1)} %param.21, bf16[768,3072]{1,0:T(8,128)(2,1)} %param.20, f32[768]{0:T(1024)S(1)} %copy-done.15, f32[144]{0:T(256)S(1)} %add_rsqrt_fusion, f32[144]{0:T(256)S(1)} %broadcast_multiply_fusion), kind=kOutput, calls=%fused_computation.38 | convolution fusion | flops 1363599360 | bytes 10104960 | tf_op jit(solution)/shard_map/dot_general | solution.py:110
  (337 shorter events, 209.5 us)
Async XLA Ops:
  6.5 92.4 %copy-start = (bf16[768,2304]{1,0:T(8,128)(2,1)S(1)}, bf16[768,2304]{1,0:T(8,128)(2,1)}, u32[]{:S(2)}) copy-start(bf16[768,2304]{1,0:T(8,128)(2,1)} %param.16) | copy-start | bytes 10616836
  6.5 91.0 %reduce-scatter.4.cloned.1.call-start = ((), (), s32[]{:S(2)}) async-start(), calls=%async_computation.5 | async-start | bytes 3981312 | tf_op jit(solution)/shard_map/reduce_scatter | solution.py:36
  15.6 83.3 %copy-start.13 = (f32[768]{0:T(1024)S(1)}, f32[768]{0:T(1024)}, u32[]{:S(2)}) copy-start(f32[768]{0:T(1024)} %param.15) | copy-start | bytes 9220
  15.6 84.8 %copy-start.16 = (f32[12]{0:T(128)S(1)}, f32[12]{0:T(128)}, u32[]{:S(2)}) copy-start(f32[12]{0:T(128)} %param.17) | copy-start | bytes 148
  15.6 130.9 %all-gather.2.cloned.1.call-start = ((), (), s32[]{:S(2)}) async-start(), calls=%async_computation.4 | async-start | bytes 1990656 | tf_op jit(solution)/shard_map/all_gather | solution.py:45
  154.6 11.7 %collective-permute-start = (bf16[2,144,768]{2,1,0:T(8,128)(2,1)}, bf16[2,144,768]{2,1,0:T(8,128)(2,1)}, u32[]{:S(2)}, u32[]{:S(2)}) collective-permute-start(bf16[2,144,768]{2,1,0:T(8,128)(2,1)} %get-tuple-element.170), channel_id=1, source_target_pairs={{0,8},{8,16},{16,24},{24,32},{32,40},{40,48},{48,56},{56,64},{64,7... | collective-permute-start | bytes 1327112 | tf_op jit(solution)/shard_map/while/body/eval_jaxpr/ppermute | solution.py:10
  171.9 3.1 copy-start.5
  176.5 3.2 copy-start.7
  181.6 11.7 %collective-permute-start = (bf16[2,144,768]{2,1,0:T(8,128)(2,1)}, bf16[2,144,768]{2,1,0:T(8,128)(2,1)}, u32[]{:S(2)}, u32[]{:S(2)}) collective-permute-start(bf16[2,144,768]{2,1,0:T(8,128)(2,1)} %get-tuple-element.170), channel_id=1, source_target_pairs={{0,8},{8,16},{16,24},{24,32},{32,40},{40,48},{48,56},{56,64},{64,7... | collective-permute-start | bytes 1327112 | tf_op jit(solution)/shard_map/while/body/eval_jaxpr/ppermute | solution.py:10
  198.8 3.0 copy-start.5
  203.4 3.2 copy-start.7
  208.4 11.7 %collective-permute-start = (bf16[2,144,768]{2,1,0:T(8,128)(2,1)}, bf16[2,144,768]{2,1,0:T(8,128)(2,1)}, u32[]{:S(2)}, u32[]{:S(2)}) collective-permute-start(bf16[2,144,768]{2,1,0:T(8,128)(2,1)} %get-tuple-element.170), channel_id=1, source_target_pairs={{0,8},{8,16},{16,24},{24,32},{32,40},{40,48},{48,56},{56,64},{64,7... | collective-permute-start | bytes 1327112 | tf_op jit(solution)/shard_map/while/body/eval_jaxpr/ppermute | solution.py:10
  225.6 3.0 copy-start.5
  230.2 3.2 copy-start.7
  235.3 11.7 %collective-permute-start = (bf16[2,144,768]{2,1,0:T(8,128)(2,1)}, bf16[2,144,768]{2,1,0:T(8,128)(2,1)}, u32[]{:S(2)}, u32[]{:S(2)}) collective-permute-start(bf16[2,144,768]{2,1,0:T(8,128)(2,1)} %get-tuple-element.170), channel_id=1, source_target_pairs={{0,8},{8,16},{16,24},{24,32},{32,40},{40,48},{48,56},{56,64},{64,7... | collective-permute-start | bytes 1327112 | tf_op jit(solution)/shard_map/while/body/eval_jaxpr/ppermute | solution.py:10
  252.5 3.0 copy-start.5
  257.1 3.2 copy-start.7
  262.1 11.7 %collective-permute-start = (bf16[2,144,768]{2,1,0:T(8,128)(2,1)}, bf16[2,144,768]{2,1,0:T(8,128)(2,1)}, u32[]{:S(2)}, u32[]{:S(2)}) collective-permute-start(bf16[2,144,768]{2,1,0:T(8,128)(2,1)} %get-tuple-element.170), channel_id=1, source_target_pairs={{0,8},{8,16},{16,24},{24,32},{32,40},{40,48},{48,56},{56,64},{64,7... | collective-permute-start | bytes 1327112 | tf_op jit(solution)/shard_map/while/body/eval_jaxpr/ppermute | solution.py:10
  279.3 3.0 copy-start.5
  283.9 3.2 copy-start.7
  289.0 11.7 %collective-permute-start = (bf16[2,144,768]{2,1,0:T(8,128)(2,1)}, bf16[2,144,768]{2,1,0:T(8,128)(2,1)}, u32[]{:S(2)}, u32[]{:S(2)}) collective-permute-start(bf16[2,144,768]{2,1,0:T(8,128)(2,1)} %get-tuple-element.170), channel_id=1, source_target_pairs={{0,8},{8,16},{16,24},{24,32},{32,40},{40,48},{48,56},{56,64},{64,7... | collective-permute-start | bytes 1327112 | tf_op jit(solution)/shard_map/while/body/eval_jaxpr/ppermute | solution.py:10
  306.2 3.0 copy-start.5
  310.8 3.2 copy-start.7
  315.8 11.7 %collective-permute-start = (bf16[2,144,768]{2,1,0:T(8,128)(2,1)}, bf16[2,144,768]{2,1,0:T(8,128)(2,1)}, u32[]{:S(2)}, u32[]{:S(2)}) collective-permute-start(bf16[2,144,768]{2,1,0:T(8,128)(2,1)} %get-tuple-element.170), channel_id=1, source_target_pairs={{0,8},{8,16},{16,24},{24,32},{32,40},{40,48},{48,56},{56,64},{64,7... | collective-permute-start | bytes 1327112 | tf_op jit(solution)/shard_map/while/body/eval_jaxpr/ppermute | solution.py:10
  333.0 3.0 copy-start.5
  337.6 3.2 copy-start.7
  342.6 11.7 %collective-permute-start = (bf16[2,144,768]{2,1,0:T(8,128)(2,1)}, bf16[2,144,768]{2,1,0:T(8,128)(2,1)}, u32[]{:S(2)}, u32[]{:S(2)}) collective-permute-start(bf16[2,144,768]{2,1,0:T(8,128)(2,1)} %get-tuple-element.170), channel_id=1, source_target_pairs={{0,8},{8,16},{16,24},{24,32},{32,40},{40,48},{48,56},{56,64},{64,7... | collective-permute-start | bytes 1327112 | tf_op jit(solution)/shard_map/while/body/eval_jaxpr/ppermute | solution.py:10
  359.8 3.0 copy-start.5
  364.5 3.2 copy-start.7
  369.5 11.7 %collective-permute-start = (bf16[2,144,768]{2,1,0:T(8,128)(2,1)}, bf16[2,144,768]{2,1,0:T(8,128)(2,1)}, u32[]{:S(2)}, u32[]{:S(2)}) collective-permute-start(bf16[2,144,768]{2,1,0:T(8,128)(2,1)} %get-tuple-element.170), channel_id=1, source_target_pairs={{0,8},{8,16},{16,24},{24,32},{32,40},{40,48},{48,56},{56,64},{64,7... | collective-permute-start | bytes 1327112 | tf_op jit(solution)/shard_map/while/body/eval_jaxpr/ppermute | solution.py:10
  386.7 3.0 copy-start.5
  391.3 3.2 copy-start.7
  396.3 11.7 %collective-permute-start = (bf16[2,144,768]{2,1,0:T(8,128)(2,1)}, bf16[2,144,768]{2,1,0:T(8,128)(2,1)}, u32[]{:S(2)}, u32[]{:S(2)}) collective-permute-start(bf16[2,144,768]{2,1,0:T(8,128)(2,1)} %get-tuple-element.170), channel_id=1, source_target_pairs={{0,8},{8,16},{16,24},{24,32},{32,40},{40,48},{48,56},{56,64},{64,7... | collective-permute-start | bytes 1327112 | tf_op jit(solution)/shard_map/while/body/eval_jaxpr/ppermute | solution.py:10
  418.1 3.2 copy-start.7
  423.2 11.7 %collective-permute-start = (bf16[2,144,768]{2,1,0:T(8,128)(2,1)}, bf16[2,144,768]{2,1,0:T(8,128)(2,1)}, u32[]{:S(2)}, u32[]{:S(2)}) collective-permute-start(bf16[2,144,768]{2,1,0:T(8,128)(2,1)} %get-tuple-element.170), channel_id=1, source_target_pairs={{0,8},{8,16},{16,24},{24,32},{32,40},{40,48},{48,56},{56,64},{64,7... | collective-permute-start | bytes 1327112 | tf_op jit(solution)/shard_map/while/body/eval_jaxpr/ppermute | solution.py:10
  445.0 3.2 copy-start.7
  450.0 11.7 %collective-permute-start = (bf16[2,144,768]{2,1,0:T(8,128)(2,1)}, bf16[2,144,768]{2,1,0:T(8,128)(2,1)}, u32[]{:S(2)}, u32[]{:S(2)}) collective-permute-start(bf16[2,144,768]{2,1,0:T(8,128)(2,1)} %get-tuple-element.170), channel_id=1, source_target_pairs={{0,8},{8,16},{16,24},{24,32},{32,40},{40,48},{48,56},{56,64},{64,7... | collective-permute-start | bytes 1327112 | tf_op jit(solution)/shard_map/while/body/eval_jaxpr/ppermute | solution.py:10
  471.8 3.2 copy-start.7
  476.9 11.7 %collective-permute-start = (bf16[2,144,768]{2,1,0:T(8,128)(2,1)}, bf16[2,144,768]{2,1,0:T(8,128)(2,1)}, u32[]{:S(2)}, u32[]{:S(2)}) collective-permute-start(bf16[2,144,768]{2,1,0:T(8,128)(2,1)} %get-tuple-element.170), channel_id=1, source_target_pairs={{0,8},{8,16},{16,24},{24,32},{32,40},{40,48},{48,56},{56,64},{64,7... | collective-permute-start | bytes 1327112 | tf_op jit(solution)/shard_map/while/body/eval_jaxpr/ppermute | solution.py:10
  498.7 3.2 copy-start.7
  503.7 11.7 %collective-permute-start = (bf16[2,144,768]{2,1,0:T(8,128)(2,1)}, bf16[2,144,768]{2,1,0:T(8,128)(2,1)}, u32[]{:S(2)}, u32[]{:S(2)}) collective-permute-start(bf16[2,144,768]{2,1,0:T(8,128)(2,1)} %get-tuple-element.170), channel_id=1, source_target_pairs={{0,8},{8,16},{16,24},{24,32},{32,40},{40,48},{48,56},{56,64},{64,7... | collective-permute-start | bytes 1327112 | tf_op jit(solution)/shard_map/while/body/eval_jaxpr/ppermute | solution.py:10
  525.5 3.2 copy-start.7
  530.6 11.7 %collective-permute-start = (bf16[2,144,768]{2,1,0:T(8,128)(2,1)}, bf16[2,144,768]{2,1,0:T(8,128)(2,1)}, u32[]{:S(2)}, u32[]{:S(2)}) collective-permute-start(bf16[2,144,768]{2,1,0:T(8,128)(2,1)} %get-tuple-element.170), channel_id=1, source_target_pairs={{0,8},{8,16},{16,24},{24,32},{32,40},{40,48},{48,56},{56,64},{64,7... | collective-permute-start | bytes 1327112 | tf_op jit(solution)/shard_map/while/body/eval_jaxpr/ppermute | solution.py:10
  552.4 3.2 copy-start.7
  569.5 15.3 %all-to-all-start.1 = ((f32[8,1,1728]{2,1,0:T(1,128)}), f32[8,1,1728]{2,1,0:T(1,128)}, u32[]{:S(2)}, u32[]{:S(2)}) async-start(f32[8,1,1728]{2,1,0:T(1,128)} %reshape.92), calls=%async_computation.1 | async-start | bytes 114688 | tf_op jit(solution)/shard_map/all_to_all | solution.py:94
  584.8 12.1 %all-to-all-start.2 = ((f32[8,1,1728]{2,1,0:T(1,128)}), f32[8,1,1728]{2,1,0:T(1,128)}, u32[]{:S(2)}, u32[]{:S(2)}) async-start(f32[8,1,1728]{2,1,0:T(1,128)} %reshape.94), calls=%async_computation.2 | async-start | bytes 114688 | tf_op jit(solution)/shard_map/all_to_all | solution.py:95
  596.9 37.8 %all-to-all-start = ((f32[1,1152,768]{2,0,1:T(1,128)}), f32[1,1152,768]{2,0,1:T(1,128)}, u32[]{:S(2)}, u32[]{:S(2)}) async-start(f32[1,1152,768]{2,0,1:T(1,128)} %copy.44), calls=%async_computation | async-start | bytes 7077888 | tf_op jit(solution)/shard_map/all_to_all | solution.py:87
  639.9 6.7 %copy-start.1 = (bf16[768,2304]{1,0:T(8,128)(2,1)S(1)}, bf16[768,2304]{1,0:T(8,128)(2,1)}, u32[]{:S(2)}) copy-start(bf16[768,2304]{1,0:T(8,128)(2,1)} %param.16) | copy-start | bytes 10616836
  (45 other events, 88.4 us)
Sparse Core Ops, SparseCore 0:
  15.7 81.7 reduce-scatter.3
  100.6 45.8 all-gather.1
where the time goes:
time: 657 us; the launch traced here: 653 us
  waiting for transfers between devices  315 us (48%)
  local copies, waits for them, and re-layouts  162 us (25%)
  matrix products  98.3 us (15%)
  other arithmetic  45.6 us (7%)
  starting transfers between devices  17 us (3%)
  between operations  13.7 us (2%)
    ppermute x15, waiting for transfers between devices, shifted(): return lax.ppermute(value, axis, pairs)  175 us
    reduce_scatter x1, waiting for transfers between devices, on_device(): lax.psum_scatter(contract_first(tile_embeds, w_eff), 'grp', scatter_dimen...  81.9 us
    slice x30, local copies, waits for them, and re-layouts, absorb(): value_heads = kv_block[1].reshape(row_count, head_count, head_size)  55.3 us
    dot_general x16, matrix products, absorb(): jnp.einsum('qhd,khd->qhk', block_queries, key_heads, preferred_element_ty...  47 us
    all_gather x1, waiting for transfers between devices, on_device(): lax.all_gather(query, 'grp', axis=0, tiled=True)  44.1 us
    dot_general x16, matrix products, absorb(): jnp.einsum('qhk,khd->qhd', expo.astype(jnp.bfloat16), value_heads, prefer...  39.6 us
    while x150, local copies, waits for them, and re-layouts  37.6 us
    slice x15, local copies, waits for them, and re-layouts, absorb(): key_heads = kv_block[0].reshape(row_count, head_count, head_size)  27.8 us
  transfers between devices with their start and end apart: 20, of which 19 were waited for; matrix products, arithmetic and copies ran while one was open for 5% of the time, Pallas kernels for 0%

commit v1 on v0

v1 whole, which is shorter than its diff:
```python
import functools

import jax
import jax.numpy as jnp
from jax import lax
from jax.experimental import pallas as pl
from jax.experimental.pallas import tpu as pltpu
from jax.sharding import PartitionSpec as P

MESH = pl.DeviceIdType.MESH
ANY = pl.BlockSpec(memory_space=pl.ANY)
VMEM = pl.BlockSpec(memory_space=pltpu.VMEM)
SMEM = pl.BlockSpec(memory_space=pltpu.SMEM)
BF16 = jnp.bfloat16
F32 = jnp.float32
LOG2E = 1.4426950408889634
SIDE = 4
GROUPS = 8
TEAM = 3
SIZE = 64
SHARE = TEAM * SIZE
LANES = 128
SLOTS = 8
FORWARD = {0: 1, 2: 4, 3: 5, 6: 7}
Z_SLOT = {1: 2, 3: 3, 2: 6}


def position():
    seq, grp = lax.axis_index("seq"), lax.axis_index("grp")
    x = (seq // 8) * 2 + grp % 2
    return x, (seq // 2) % 4, grp // 2, seq % 2


def device(x, y, z, core):
    return ((x // 2) * 8 + y * 2 + core, z * 2 + x % 2)


def remote(src, dst, send_sem, recv_sem, partner):
    return pltpu.make_async_remote_copy(
        src_ref=src, dst_ref=dst, send_sem=send_sem, recv_sem=recv_sem,
        device_id=partner, device_id_type=MESH,
    )


def norm_rows(floats, gain):
    average = jnp.mean(floats, axis=-1, keepdims=True)
    centred = floats - average
    spread = jnp.mean(centred * centred, axis=-1, keepdims=True)
    return (centred * lax.rsqrt(spread + 1e-05) * gain).astype(BF16)


def layer_kernel(
    embeds_hbm, w_in_hbm, perturb_hbm, gain_attn, w_qkv_hbm, temper, w_out_hbm, gain_mlp,
    w_up_hbm, w_down_hbm,
    out_ref,
    embeds, w_in, perturb, w_qkv, w_out, w_up, w_down,
    partial, arrived, q_out, kv_out, q_all, kv_all,
    turned, score_a, score_b, acc, peak, o_out, o_in, mine, back,
    load_sem, part_send, part_recv, y_send, y_recv, x_send, x_recv, z_send, kv_recv, c_send,
    o_send, o_recv, b_send, b_recv,
):
    x, y, z, core = position()
    seq, grp = lax.axis_index("seq"), lax.axis_index("grp")
    rows, width = out_ref.shape
    block = SIDE * rows
    ahead = (1, 2, 3)
    x_to = {d: device(lax.rem(x + d, SIDE), y, z, core) for d in ahead}
    y_to = {d: device(x, lax.rem(y + d, SIDE), z, core) for d in ahead}
    z_to = {d: device(x, y, lax.rem(z + d, SIDE), core) for d in ahead}
    sibling = device(x, y, z, 1 - core)
    peers = [(seq, lax.rem(grp + d, GROUPS)) for d in range(1, GROUPS)]
    far = [device(lax.rem(x + 2, SIDE), y, z, core), device(3 - x, y, z, core)]

    loads = [
        pltpu.make_async_copy(src, dst, load_sem.at[i])
        for i, (src, dst) in enumerate([
            (embeds_hbm, embeds), (w_in_hbm, w_in), (perturb_hbm, perturb), (w_qkv_hbm, w_qkv),
            (w_out_hbm, w_out), (w_up_hbm, w_up), (w_down_hbm, w_down),
        ])
    ]
    for load in loads:
        load.start()
    barrier = pltpu.get_barrier_semaphore()
    greeted = peers + [y_to[d] for d in ahead] + [sibling] + far
    for partner in greeted:
        pl.semaphore_signal(barrier, inc=1, device_id=partner, device_id_type=MESH)
    for load in loads[:3]:
        load.wait()
    w_eff = (w_in[...].astype(F32) + perturb[...].astype(F32)).astype(BF16)
    for at in range(0, partial.shape[0], LANES):
        partial[at : at + LANES, :] = lax.dot_general(
            embeds[:, at : at + LANES], w_eff, (((0,), (0,)), ((), ())),
            preferred_element_type=F32,
        ).astype(BF16)
    pl.semaphore_wait(barrier, len(greeted))

    copies = []

    def send(*args):
        copy = remote(*args)
        copy.start()
        copies.append(copy)
        return copy

    sums = {}
    for d in (1, 2, 3, 4, 5, 6, 7):
        there = lax.rem(grp + d, GROUPS)
        start = pl.multiple_of(there * rows, 16)
        sums[d] = send(
            partial.at[pl.ds(start, rows)], arrived.at[d - 1],
            part_send.at[d - 1], part_recv.at[d - 1], (seq, there),
        )
    total = partial[pl.ds(pl.multiple_of(grp * rows, 16), rows), :].astype(F32)
    for d in range(1, GROUPS):
        sums[d].wait_recv()
        total = total + arrived[d - 1].astype(F32)
    hidden = total.astype(BF16).astype(F32)
    normed = norm_rows(hidden, gain_attn[...][None, :])

    loads[3].wait()
    keys = jnp.dot(normed, w_qkv[:, width : 2 * width], preferred_element_type=F32)
    values = jnp.dot(normed, w_qkv[:, 2 * width :], preferred_element_type=F32)
    kv_y = {}
    q_y = {}

    def exchange_kv(head):
        for part in range(SIDE):
            at = part * SHARE + head * SIZE
            kv_out[head, part] = jnp.concatenate(
                [keys[:, at : at + SIZE], values[:, at : at + SIZE]], axis=1
            ).astype(BF16)
        for d in ahead:
            kv_y[head, d] = send(
                kv_out.at[head, lax.rem(y + d, SIDE)], kv_all.at[head, 0, pl.ds(d * rows, rows)],
                y_send.at[head, d - 1], y_recv.at[head, d - 1], y_to[d],
            )
        kv_all[head, 0, 0:rows] = kv_out[head, y]

    def exchange_q(tile):
        for part in range(SIDE):
            pieces = []
            for head in (2 * tile, 2 * tile + 1):
                if head < TEAM:
                    at = part * SHARE + head * SIZE
                    pieces.append(
                        query[:, at : at + SIZE]
                        * (temper[part * TEAM + head] * (SIZE ** (-0.5) * LOG2E))
                    )
                else:
                    pieces.append(jnp.zeros((rows, SIZE), F32))
            q_out[tile, part] = jnp.concatenate(pieces, axis=1).astype(BF16)
        for d in ahead:
            q_y[tile, d] = send(
                q_out.at[tile, lax.rem(y + d, SIDE)], q_all.at[tile, 0, pl.ds(d * rows, rows)],
                y_send.at[TEAM + tile, d - 1], y_recv.at[TEAM + tile, d - 1], y_to[d],
            )
        q_all[tile, 0, 0:rows] = q_out[tile, y]

    exchange_kv(0)
    query = jnp.dot(normed, w_qkv[:, :width], preferred_element_type=F32)
    exchange_q(0)
    exchange_kv(1)
    exchange_kv(2)
    exchange_q(1)

    kv_z = {}
    kv_c = {}
    q_x = {}

    def spread_kv(head):
        for d in ahead:
            kv_y[head, d].wait_recv()
        own = kv_all.at[head, 0]
        for d in (1, 3, 2):
            kv_z[head, Z_SLOT[d]] = send(
                own, kv_all.at[head, Z_SLOT[d]], z_send.at[head, d - 1],
                kv_recv.at[head, Z_SLOT[d]], z_to[d],
            )
        forward_kv(head, 0)

    def forward_kv(head, slot):
        to = FORWARD[slot]
        kv_c[head, to] = remote(
            kv_all.at[head, slot], kv_all.at[head, to], c_send.at[head, to],
            kv_recv.at[head, to], sibling,
        )
        kv_c[head, to].start()

    def spread_q(tile):
        for d in ahead:
            q_y[tile, d].wait_recv()
        for d in (1, 3, 2):
            q_x[tile, d] = send(
                q_all.at[tile, 0], q_all.at[tile, d], x_send.at[tile, d - 1],
                x_recv.at[tile, d - 1], x_to[d],
            )

    spread_kv(0)
    spread_q(0)
    spread_kv(1)
    spread_kv(2)
    spread_q(1)

    columns = turned.shape[1]
    ones = jnp.ones((8, block), BF16)
    o_x = {}
    for head in range(TEAM):
        tile, half = divmod(head, 2)
        if half == 0:
            for d in ahead:
                q_x[tile, d].wait_recv()
        for slot in range(SIDE):
            part = q_all[tile, slot].T
            turned[0:SIZE, slot * block : (slot + 1) * block] = part[half * SIZE : (half + 1) * SIZE]
        turned[SIZE:LANES, :] = jnp.zeros((LANES - SIZE, columns), BF16)
        acc[...] = jnp.zeros(acc.shape, F32)
        peak[...] = jnp.full(peak.shape, -1e30, F32)

        def score(slot, into, head=head):
            into[...] = jnp.dot(kv_all[head, slot], turned[...], preferred_element_type=F32)

        def absorb(slot, scores_ref, head=head):
            scores = scores_ref[...]
            before = peak[0:1, :]
            after = jnp.maximum(before, jnp.max(scores, axis=0, keepdims=True))
            peak[0:1, :] = after
            weights = jnp.exp2(scores - after).astype(BF16)
            both = kv_all[head, slot].T
            values = jnp.concatenate([both[SIZE:], ones], axis=0)
            acc[...] = acc[...] * jnp.exp2(before - after) + jnp.dot(
                values, weights, preferred_element_type=F32
            )

        def wait_slot(slot, head=head):
            pltpu.make_async_copy(
                kv_all.at[head, slot], kv_all.at[head, slot], kv_recv.at[head, slot]
            ).wait()

        score(0, score_a)

        def pair(step, _, head=head):
            @pl.when(step == 0)
            def _():
                wait_slot(2)
                forward_kv(head, 2)
                wait_slot(1)

            @pl.when(step == 1)
            def _():
                wait_slot(3)
                forward_kv(head, 3)
                wait_slot(4)

            @pl.when(step == 2)
            def _():
                wait_slot(6)
                forward_kv(head, 6)
                wait_slot(5)

            @pl.when(step == 3)
            def _():
                wait_slot(7)

            score(2 * step + 1, score_b)
            absorb(2 * step, score_a)
            score(jnp.minimum(2 * step + 2, SLOTS - 1), score_a)
            absorb(2 * step + 1, score_b)
            return 0

        lax.fori_loop(0, SLOTS // 2, pair, 0)

        sums_row = acc[SIZE : SIZE + 1, :]
        log_sum = peak[0:1, :] + jnp.log2(sums_row)
        high = log_sum.astype(BF16).astype(F32)
        low = log_sum - high
        whole = jnp.concatenate(
            [
                acc[0:SIZE, :] * (1.0 / sums_row),
                jnp.broadcast_to(high, (8, columns)),
                jnp.broadcast_to(low, (8, columns)),
                jnp.zeros((LANES - SIZE - 16, columns), F32),
            ],
            axis=0,
        )
        for slot in (1, 3, 2, 0):
            o_out[head, slot] = whole[:, slot * block : (slot + 1) * block].T.astype(BF16)
            if slot:
                o_x[head, slot] = send(
                    o_out.at[head, slot], o_in.at[head, slot - 1], o_send.at[head, slot - 1],
                    o_recv.at[head, slot - 1], x_to[SIDE - slot],
                )

    def merge(head):
        for slot in ahead:
            o_x[head, slot].wait_recv()
        pieces = [o_out[head, 0].astype(F32)]
        pieces += [o_in[head, slot - 1].astype(F32) for slot in ahead]
        logs = [piece[:, SIZE : SIZE + 1] + piece[:, SIZE + 8 : SIZE + 9] for piece in pieces]
        top = functools.reduce(jnp.maximum, logs)
        shares = [jnp.exp2(log - top) for log in logs]
        inverse = 1.0 / functools.reduce(jnp.add, shares)
        return functools.reduce(
            jnp.add,
            [piece[:, :SIZE] * (one * inverse) for piece, one in zip(pieces, shares)],
        )

    b_y = {}

    def give_back(tile, value):
        mine[tile] = value.astype(BF16)
        for d in ahead:
            b_y[tile, d] = send(
                mine.at[tile, pl.ds(d * rows, rows)], back.at[tile, d],
                b_send.at[tile, d - 1], b_recv.at[tile, d - 1], y_to[SIDE - d],
            )

    give_back(0, jnp.concatenate([merge(0), merge(1)], axis=1))
    give_back(1, jnp.concatenate([merge(2), jnp.zeros((block, SIZE), F32)], axis=1))
    mixed = hidden
    loads[4].wait()
    for tile in range(2):
        used = LANES if tile == 0 else SIZE
        for d in range(SIDE):
            if d:
                b_y[tile, d].wait_recv()
                piece = back[tile, d]
            else:
                piece = mine[tile, 0:rows]
            owner = lax.rem(y + d, SIDE)
            start = pl.multiple_of(owner * SHARE + tile * LANES, 16)
            mixed = mixed + jnp.dot(
                piece[:, :used], w_out[pl.ds(start, used), :], preferred_element_type=F32
            )
    resid = mixed.astype(BF16).astype(F32)
    normed = norm_rows(resid, gain_mlp[...][None, :])
    loads[5].wait()
    loads[6].wait()
    encoded = resid
    for at in range(0, w_up.shape[1], width):
        raised = jnp.dot(normed, w_up[:, at : at + width], preferred_element_type=F32)
        active = jax.nn.gelu(raised).astype(BF16)
        encoded = encoded + jnp.dot(active, w_down[at : at + width, :], preferred_element_type=F32)
    out_ref[...] = encoded.astype(BF16)
    for copy in copies:
        copy.wait_send()
    for head in range(TEAM):
        for slot, to in FORWARD.items():
            pltpu.make_async_copy(
                kv_all.at[head, slot], kv_all.at[head, slot], c_send.at[head, to]
            ).wait()


def on_device(tile_embeds, w_in, perturb, gain_attn, w_qkv, temper, w_out, gain_mlp, w_up, w_down):
    width = w_qkv.shape[0]
    rows = tile_embeds.shape[1] // GROUPS
    block = SIDE * rows
    columns = SIDE * block
    dma = pltpu.SemaphoreType.DMA
    vmem = pltpu.VMEM
    return pl.pallas_call(
        layer_kernel,
        out_shape=jax.ShapeDtypeStruct((rows, width), BF16),
        in_specs=[ANY, ANY, ANY, VMEM, ANY, SMEM, ANY, VMEM, ANY, ANY],
        out_specs=VMEM,
        scratch_shapes=[
            vmem(tile_embeds.shape, BF16), vmem(w_in.shape, BF16), vmem(perturb.shape, BF16),
            vmem(w_qkv.shape, BF16), vmem(w_out.shape, BF16), vmem(w_up.shape, BF16),
            vmem(w_down.shape, BF16),
            vmem((GROUPS * rows, width), BF16),
            vmem((GROUPS - 1, rows, width), BF16),
            vmem((2, SIDE, rows, LANES), BF16),
            vmem((TEAM, SIDE, rows, LANES), BF16),
            vmem((2, SIDE, block, LANES), BF16),
            vmem((TEAM, SLOTS, block, LANES), BF16),
            vmem((LANES, columns), BF16),
            vmem((block, columns), F32),
            vmem((block, columns), F32),
            vmem((SIZE + 8, columns), F32),
            vmem((8, columns), F32),
            vmem((TEAM, SIDE, block, LANES), BF16),
            vmem((TEAM, SIDE - 1, block, LANES), BF16),
            vmem((2, block, LANES), BF16),
            vmem((2, SIDE, rows, LANES), BF16),
            dma((7,)), dma((7,)), dma((7,)), dma((5, 3)), dma((5, 3)), dma((2, 3)), dma((2, 3)),
            dma((TEAM, 3)), dma((TEAM, SLOTS)), dma((TEAM, SLOTS)),
            dma((TEAM, 3)), dma((TEAM, 3)), dma((2, 3)), dma((2, 3)),
        ],
        compiler_params=pltpu.CompilerParams(
            collective_id=0, has_side_effects=True, vmem_limit_bytes=56 * 2**20
        ),
        name="layer",
    )(tile_embeds, w_in, perturb, gain_attn, w_qkv, temper, w_out, gain_mlp, w_up, w_down)


def solution(mesh):
    placed = (P("grp", "seq"), P("grp", None), P("grp", None), P(), P(), P(), P(), P(), P(), P())
    return jax.shard_map(
        on_device, mesh=mesh, in_specs=placed, out_specs=P(("seq", "grp"), None), check_vma=False
    )
```

time: 657 us -> 103 us (0.16)
  waiting for transfers between devices: 315 us -> 0 us
  local copies, waits for them, and re-layouts: 162 us -> 1.64 us
  Pallas kernels: 0 us -> 101 us
  matrix products: 98.3 us -> 0 us
  other arithmetic: 45.6 us -> 0 us
  starting transfers between devices: 17 us -> 0 us
  between operations: 13.7 us -> 0.01 us
    ppermute x15 -> x0, waiting for transfers between devices: 175 us -> none  [shifted(): return lax.ppermute(value, axis, pairs)]
    pallas_call x0 -> x1, Pallas kernels: none -> 101 us  [on_device(): pl.pallas_call(layer_kernel, out_shape=jax.ShapeDtypeStruct((rows, width)...]
    dot_general x36 -> x0, matrix products: 98.3 us -> none  [the longest x16 47 us: absorb(): jnp.einsum('qhd,khd->qhk', block_queries, key_heads, preferred_element_ty...]
    slice x47 -> x0, local copies, waits for them, and re-layouts: 84.2 us -> none  [the longest x30 55.3 us: absorb(): value_heads = kv_block[1].reshape(row_count, head_count, head_size)]
    reduce_scatter x1 -> x0, waiting for transfers between devices: 81.9 us -> none  [on_device(): lax.psum_scatter(contract_first(tile_embeds, w_eff), 'grp', scatter_dimen...]
    all_gather x1 -> x0, waiting for transfers between devices: 44.1 us -> none  [on_device(): lax.all_gather(query, 'grp', axis=0, tiled=True)]
    while x152 -> x0, local copies, waits for them, and re-layouts: 41.5 us -> none
    reduce_sum x21 -> x0, other arithmetic: 25.3 us -> none  [the longest x16 23.1 us: absorb(): new_sum = running_sum * rescale + jnp.sum(expo, axis=-1)]
  transfers between devices with their start and end apart: 20 -> 0, of which waited for: 19 -> 0; matrix products, arithmetic and copies ran while one was open for 5% -> 0% of each run, Pallas kernels for 0% -> 0%
where the time goes in v1:
time: 103 us; the launch traced here: 102 us
  Pallas kernels  101 us (98%)
  local copies, waits for them, and re-layouts  1.64 us (2%)
    pallas_call x1, Pallas kernels, on_device(): pl.pallas_call(layer_kernel, out_shape=jax.ShapeDtypeStruct((rows, width)...  101 us

profile of v1, /device:TPU:0, one launch (start us, length us, event | category | flops | bytes accessed | tf_op | source)
XLA Modules:
  0.0 102.5 jit_solution(4915152172494338841)
XLA Ops:
  0.0 100.8 %layer.1 = bf16[144,768]{1,0:T(8,128)(2,1)} custom-call(bf16[192,1152]{1,0:T(8,128)(2,1)} %embeds_hbm.1, bf16[192,768]{1,0:T(8,128)(2,1)} %w_in_hbm.1, bf16[192,768]{1,0:T(8,128)(2,1)} %perturb_hbm.1, f32[768]{0:T(1024)} %gain_attn.1, bf16[768,2304]{1,0:T(8,128)(2,1)} %w_qkv_hbm.1, f32[12]{0:T(128)} %temper.1, bf16[768,768]{1,0:T(8,128)(2,1)} %w_out_hbm.1, ...), custom_call_target="tpu_custom_call" | custom-call | tf_op jit(solution)/shard_map/layer/pallas_call | solution.py:360
  100.8 1.6 %copy.12 = bf16[144,768]{1,0:T(8,128)(2,1)} copy(bf16[144,768]{1,0:T(8,128)(2,1)} %layer.1) | data formatting | bytes 442368

commit v2 on v1

v2 whole, which is shorter than its diff:
```python
import functools

import jax
import jax.numpy as jnp
from jax import lax
from jax.experimental import pallas as pl
from jax.experimental.pallas import tpu as pltpu
from jax.sharding import PartitionSpec as P

MESH = pl.DeviceIdType.MESH
ANY = pl.BlockSpec(memory_space=pl.ANY)
VMEM = pl.BlockSpec(memory_space=pltpu.VMEM)
SMEM = pl.BlockSpec(memory_space=pltpu.SMEM)
BF16 = jnp.bfloat16
F32 = jnp.float32
LOG2E = 1.4426950408889634
SIDE = 4
GROUPS = 8
TEAM = 3
SIZE = 64
SHARE = TEAM * SIZE
LANES = 128
SLOTS = 8
FOLD = 80
STRIP = 256
FORWARD = {0: 1, 2: 4, 3: 5, 6: 7}
Z_SLOT = {1: 2, 3: 3, 2: 6}


def position():
    seq, grp = lax.axis_index("seq"), lax.axis_index("grp")
    x = (seq // 8) * 2 + grp % 2
    return x, (seq // 2) % 4, grp // 2, seq % 2


def device(x, y, z, core):
    return ((x // 2) * 8 + y * 2 + core, z * 2 + x % 2)


def remote(src, dst, send_sem, recv_sem, partner):
    return pltpu.make_async_remote_copy(
        src_ref=src, dst_ref=dst, send_sem=send_sem, recv_sem=recv_sem,
        device_id=partner, device_id_type=MESH,
    )


def fold(piece):
    rows = piece.shape[0]
    blank = jnp.zeros((2 * FOLD - rows, SIZE), piece.dtype)
    lower = jnp.concatenate([piece[FOLD:], blank], axis=0)
    return jnp.concatenate([piece[:FOLD], lower], axis=1).astype(BF16)


def unfold(folded, rows):
    pieces = []
    for at in range(0, folded.shape[0], FOLD):
        pieces += [folded[at : at + FOLD, :SIZE], folded[at : at + rows - FOLD, SIZE:]]
    return jnp.concatenate(pieces, axis=0)


def norm_rows(floats, gain):
    average = jnp.mean(floats, axis=-1, keepdims=True)
    centred = floats - average
    spread = jnp.mean(centred * centred, axis=-1, keepdims=True)
    return (centred * lax.rsqrt(spread + 1e-05) * gain).astype(BF16)


def layer_kernel(
    embeds_hbm, w_in_hbm, perturb_hbm, gain_attn, w_qkv_hbm, temper, w_out_hbm, gain_mlp,
    w_up_hbm, w_down_hbm,
    out_ref,
    embeds, w_in, perturb, w_qkv, w_out, w_up, w_down,
    w_all, embed_out, embed_all, partial, arrived, q_out, kv_out, q_all, kv_all,
    turned, score_a, score_b, acc, peak, o_out, o_in, l_out, l_in, mine, back,
    load_sem, w_send, w_recv, e_send, e_recv, part_send, part_recv, y_send, y_recv, x_send, x_recv, z_send, kv_recv, c_send,
    o_send, o_recv, b_send, b_recv,
):
    x, y, z, core = position()
    rows, width = out_ref.shape
    block = SIDE * rows
    ahead = (1, 2, 3)
    x_to = {d: device(lax.rem(x + d, SIDE), y, z, core) for d in ahead}
    y_to = {d: device(x, lax.rem(y + d, SIDE), z, core) for d in ahead}
    z_to = {d: device(x, y, lax.rem(z + d, SIDE), core) for d in ahead}
    sibling = device(x, y, z, 1 - core)
    loads = [
        pltpu.make_async_copy(src, dst, load_sem.at[i])
        for i, (src, dst) in enumerate([
            (embeds_hbm, embeds), (w_in_hbm, w_in), (perturb_hbm, perturb), (w_qkv_hbm, w_qkv),
            (w_out_hbm, w_out), (w_up_hbm, w_up), (w_down_hbm, w_down),
        ])
    ]
    for load in loads:
        load.start()
    barrier = pltpu.get_barrier_semaphore()
    greeted = [to[d] for to in (x_to, y_to, z_to) for d in ahead] + [sibling]
    for partner in greeted:
        pl.semaphore_signal(barrier, inc=1, device_id=partner, device_id_type=MESH)
    copies = []

    def send(*args):
        copy = remote(*args)
        copy.start()
        copies.append(copy)
        return copy

    for load in loads[1:3]:
        load.wait()
    half = width // 2
    w_eff = (w_in[...].astype(F32) + perturb[...].astype(F32)).astype(BF16)
    for side in range(2):
        w_all[0, side] = w_eff[:, side * half : (side + 1) * half]
    pl.semaphore_wait(barrier, len(greeted))
    w_z, w_c = {}, {}
    for d in (1, 3, 2):
        w_z[d] = send(
            w_all.at[0, core], w_all.at[d, core], w_send.at[d - 1], w_recv.at[d - 1], z_to[d]
        )
    loads[0].wait()
    pair = 2 * rows
    x_low = lax.rem(x, 2)
    rest = w_in.shape[0] - LANES
    for there in range(SIDE):
        at = there * pair
        low = embeds[LANES:, at : at + pair]
        low = jnp.concatenate([low[:, :rows], low[:, rows:]], axis=0)
        low = jnp.concatenate([low, jnp.zeros((2 * rest, 2 * LANES - rows), BF16)], axis=1)
        top = embeds[0:LANES, at : at + pair].T
        for which in range(2):
            start = pl.multiple_of(jnp.where(x_low == which, pair, 0), 16)
            embed_out[there, pl.ds(start, rows)] = top[which * rows : (which + 1) * rows]
        embed_out[there, rows:pair] = low.T[:rows]
    e_z = {}
    for late, area in enumerate((slice(0, pair), slice(pair, pair + rows))):
        for d in (1, 3, 2):
            e_z[late, d] = send(
                embed_out.at[lax.rem(z + d, SIDE), area], embed_all.at[d - 1, area],
                e_send.at[late, d - 1], e_recv.at[late, d - 1], z_to[d],
            )
    for d in (1, 3, 2):
        w_z[d].wait_recv()
        w_c[d] = send(
            w_all.at[d, core], w_all.at[d, core], w_send.at[d + 2], w_recv.at[d + 2], sibling
        )
    lane = lax.broadcasted_iota(jnp.int32, (rows, LANES), 1)

    def part_sum(late, side):
        which = x_low if late else 1 - x_low
        summed = None
        for d in (0, 1, 3, 2):
            features = embed_out.at[z] if d == 0 else embed_all.at[d - 1]
            first = features[pair : pair + rows, :] if late else features[0:rows, :]
            second = features[rows:pair, :]
            second = jnp.where(lane // rest == which, second, jnp.zeros((), BF16))
            weight = w_all[d, side]
            weight = jnp.concatenate([weight, weight[LANES:]], axis=0)
            term = jnp.dot(
                jnp.concatenate([first, second], axis=1), weight, preferred_element_type=F32
            )
            summed = term if summed is None else summed + term
        return summed

    for d in (1, 3, 2):
        w_c[d].wait_recv()
    for d in (1, 3, 2):
        e_z[0, d].wait_recv()
    given = []
    partner = device(x + 1 - 2 * x_low, y, z, core)
    for side in range(2):
        partial[side] = part_sum(False, side).astype(BF16)
        given.append(send(
            partial.at[side], arrived.at[side], part_send.at[side], part_recv.at[side], partner
        ))
    for d in (1, 3, 2):
        e_z[1, d].wait_recv()
    own = [part_sum(True, side) for side in range(2)]
    for side in range(2):
        given[side].wait_recv()
        own[side] = own[side] + arrived[side].astype(F32)
    hidden = jnp.concatenate(own, axis=1).astype(BF16).astype(F32)
    normed = norm_rows(hidden, gain_attn[...][None, :])

    loads[3].wait()
    kv_y = {}
    q_y = {}

    def exchange_kv(head):
        for part in range(SIDE):
            at = part * SHARE + head * SIZE
            kv_out[head, part] = jnp.concatenate(
                [keys[:, at : at + SIZE], values[:, at : at + SIZE]], axis=1
            ).astype(BF16)
        for d in ahead:
            kv_y[head, d] = send(
                kv_out.at[head, lax.rem(y + d, SIDE)], kv_all.at[head, 0, pl.ds(d * rows, rows)],
                y_send.at[head, d - 1], y_recv.at[head, d - 1], y_to[d],
            )
        kv_all[head, 0, 0:rows] = kv_out[head, y]

    def exchange_q(head):
        for part in range(SIDE):
            at = part * SHARE + head * SIZE
            piece = query[:, at : at + SIZE] * (
                temper[part * TEAM + head] * (SIZE ** (-0.5) * LOG2E)
            )
            q_out[head, part] = fold(piece)
        for d in ahead:
            q_y[head, d] = send(
                q_out.at[head, lax.rem(y + d, SIDE)], q_all.at[head, 0, pl.ds(d * FOLD, FOLD)],
                y_send.at[TEAM + head, d - 1], y_recv.at[TEAM + head, d - 1], y_to[d],
            )
        q_all[head, 0, 0:FOLD] = q_out[head, y]

    query = jnp.dot(normed, w_qkv[:, :width], preferred_element_type=F32)
    exchange_q(0)
    keys = jnp.dot(normed, w_qkv[:, width : 2 * width], preferred_element_type=F32)
    values = jnp.dot(normed, w_qkv[:, 2 * width :], preferred_element_type=F32)
    exchange_kv(0)
    exchange_kv(1)
    exchange_q(1)
    exchange_kv(2)
    exchange_q(2)

    kv_z = {}
    kv_c = {}
    q_x = {}

    def spread_kv(head):
        for d in ahead:
            kv_y[head, d].wait_recv()
        own = kv_all.at[head, 0]
        for d in (1, 3, 2):
            kv_z[head, Z_SLOT[d]] = send(
                own, kv_all.at[head, Z_SLOT[d]], z_send.at[head, d - 1],
                kv_recv.at[head, Z_SLOT[d]], z_to[d],
            )
        forward_kv(head, 0)

    def forward_kv(head, slot):
        to = FORWARD[slot]
        kv_c[head, to] = remote(
            kv_all.at[head, slot], kv_all.at[head, to], c_send.at[head, to],
            kv_recv.at[head, to], sibling,
        )
        kv_c[head, to].start()

    def spread_q(head):
        for d in ahead:
            q_y[head, d].wait_recv()
        for d in (1, 3, 2):
            q_x[head, d] = send(
                q_all.at[head, 0], q_all.at[head, d], x_send.at[head, d - 1],
                x_recv.at[head, d - 1], x_to[d],
            )

    spread_q(0)
    spread_kv(0)
    spread_kv(1)
    spread_q(1)
    spread_kv(2)
    spread_q(2)

    columns = turned.shape[1]
    ones = jnp.ones((8, block), BF16)
    o_x, l_x = {}, {}
    for head in range(TEAM):
        for d in ahead:
            q_x[head, d].wait_recv()
        for slot in range(SIDE):
            part = unfold(q_all.at[head, slot], rows)
            part = jnp.concatenate([part, jnp.zeros((block, LANES - SIZE), BF16)], axis=1)
            turned[:, slot * block : (slot + 1) * block] = part.T
        acc[...] = jnp.zeros(acc.shape, F32)
        peak[...] = jnp.full(peak.shape, -1e30, F32)

        strips = [slice(at, at + STRIP) for at in range(0, columns, STRIP)]

        def score(slot, into, strip, head=head):
            into[:, strip] = jnp.dot(
                kv_all[head, slot], turned[:, strip], preferred_element_type=F32
            )

        def absorb(values, scores_ref, strip):
            scores = scores_ref[:, strip]
            before = peak[0:1, strip]
            after = jnp.maximum(before, jnp.max(scores, axis=0, keepdims=True))
            peak[0:1, strip] = after
            weights = jnp.exp2(scores - after).astype(BF16)
            acc[:, strip] = acc[:, strip] * jnp.exp2(before - after) + jnp.dot(
                values, weights, preferred_element_type=F32
            )

        def step_over(slot, now, later, into, head=head):
            values = jnp.concatenate([kv_all[head, slot].T[SIZE:], ones], axis=0)
            for strip in strips:
                score(later, into, strip)
                absorb(values, now, strip)

        def wait_slot(slot, head=head):
            pltpu.make_async_copy(
                kv_all.at[head, slot], kv_all.at[head, slot], kv_recv.at[head, slot]
            ).wait()

        for strip in strips:
            score(0, score_a, strip)

        def pair(step, _, head=head):
            @pl.when(step == 0)
            def _():
                wait_slot(2)
                forward_kv(head, 2)
                wait_slot(1)

            @pl.when(step == 1)
            def _():
                wait_slot(3)
                forward_kv(head, 3)
                wait_slot(4)

            @pl.when(step == 2)
            def _():
                wait_slot(6)
                forward_kv(head, 6)
                wait_slot(5)

            @pl.when(step == 3)
            def _():
                wait_slot(7)

            step_over(2 * step, score_a, 2 * step + 1, score_b)
            step_over(2 * step + 1, score_b, jnp.minimum(2 * step + 2, SLOTS - 1), score_a)
            return 0

        lax.fori_loop(0, SLOTS // 2, pair, 0)

        sums_row = acc[SIZE : SIZE + 1, :]
        log_sum = peak[0:1, :] + jnp.log2(sums_row)
        whole = jnp.concatenate(
            [acc[0:SIZE, :] * (1.0 / sums_row), jnp.zeros((LANES - SIZE, columns), F32)], axis=0
        )
        for slot in (1, 3, 2, 0):
            area = slice(slot * block, (slot + 1) * block)
            upright = whole[:, area].T[:, :SIZE]
            for d in range(SIDE):
                o_out[head, slot, d * FOLD : (d + 1) * FOLD] = fold(
                    upright[d * rows : (d + 1) * rows]
                )
            spare = l_out.shape[3] - block
            line = jnp.concatenate([log_sum[:, area], jnp.zeros((1, spare), F32)], axis=1)
            l_out[head, slot] = jnp.broadcast_to(line, l_out.shape[2:])
            if slot:
                to = x_to[SIDE - slot]
                o_x[head, slot] = send(
                    o_out.at[head, slot], o_in.at[head, slot - 1], o_send.at[head, slot - 1],
                    o_recv.at[head, slot - 1], to,
                )
                l_x[head, slot] = send(
                    l_out.at[head, slot], l_in.at[head, slot - 1], o_send.at[head, slot + 2],
                    o_recv.at[head, slot + 2], to,
                )

    def merge(head):
        for slot in ahead:
            o_x[head, slot].wait_recv()
            l_x[head, slot].wait_recv()
        logs = [l_out[head, 0, 0:1]] + [l_in[head, slot - 1, 0:1] for slot in ahead]
        top = functools.reduce(jnp.maximum, logs)
        shares = [jnp.exp2(log - top) for log in logs]
        inverse = 1.0 / functools.reduce(jnp.add, shares)
        shares = [share * inverse for share in shares]
        shares = jnp.concatenate(shares + shares, axis=0).T
        pieces = [o_out.at[head, 0]] + [o_in.at[head, slot - 1] for slot in ahead]
        return functools.reduce(
            jnp.add,
            [
                unfold(piece, rows).astype(F32) * shares[:block, i : i + 1]
                for i, piece in enumerate(pieces)
            ],
        )

    b_y = {}

    def give_back(tile, value):
        mine[tile] = value.astype(BF16)
        for d in ahead:
            b_y[tile, d] = send(
                mine.at[tile, pl.ds(d * rows, rows)], back.at[tile, d],
                b_send.at[tile, d - 1], b_recv.at[tile, d - 1], y_to[SIDE - d],
            )

    give_back(0, jnp.concatenate([merge(0), merge(1)], axis=1))
    give_back(1, jnp.concatenate([merge(2), jnp.zeros((block, SIZE), F32)], axis=1))
    mixed = hidden
    loads[4].wait()
    for tile in range(2):
        used = LANES if tile == 0 else SIZE
        for d in range(SIDE):
            if d:
                b_y[tile, d].wait_recv()
                piece = back[tile, d]
            else:
                piece = mine[tile, 0:rows]
            owner = lax.rem(y + d, SIDE)
            start = pl.multiple_of(owner * SHARE + tile * LANES, 16)
            mixed = mixed + jnp.dot(
                piece[:, :used], w_out[pl.ds(start, used), :], preferred_element_type=F32
            )
    resid = mixed.astype(BF16).astype(F32)
    normed = norm_rows(resid, gain_mlp[...][None, :])
    loads[5].wait()
    loads[6].wait()
    encoded = resid
    for at in range(0, w_up.shape[1], width):
        raised = jnp.dot(normed, w_up[:, at : at + width], preferred_element_type=F32)
        active = jax.nn.gelu(raised).astype(BF16)
        encoded = encoded + jnp.dot(active, w_down[at : at + width, :], preferred_element_type=F32)
    out_ref[...] = encoded.astype(BF16)
    for copy in copies:
        copy.wait_send()
    for head in range(TEAM):
        for slot, to in FORWARD.items():
            pltpu.make_async_copy(
                kv_all.at[head, slot], kv_all.at[head, slot], c_send.at[head, to]
            ).wait()


def on_device(tile_embeds, w_in, perturb, gain_attn, w_qkv, temper, w_out, gain_mlp, w_up, w_down):
    width = w_qkv.shape[0]
    rows = tile_embeds.shape[1] // GROUPS
    block = SIDE * rows
    columns = SIDE * block
    dma = pltpu.SemaphoreType.DMA
    vmem = pltpu.VMEM
    return pl.pallas_call(
        layer_kernel,
        out_shape=jax.ShapeDtypeStruct((rows, width), BF16),
        in_specs=[ANY, ANY, ANY, VMEM, ANY, SMEM, ANY, VMEM, ANY, ANY],
        out_specs=VMEM,
        scratch_shapes=[
            vmem(tile_embeds.shape, BF16), vmem(w_in.shape, BF16), vmem(perturb.shape, BF16),
            vmem(w_qkv.shape, BF16), vmem(w_out.shape, BF16), vmem(w_up.shape, BF16),
            vmem(w_down.shape, BF16),
            vmem((SIDE, 2, w_in.shape[0], width // 2), BF16),
            vmem((SIDE, 3 * rows, LANES), BF16),
            vmem((SIDE - 1, 3 * rows, LANES), BF16),
            vmem((2, rows, width // 2), BF16),
            vmem((2, rows, width // 2), BF16),
            vmem((TEAM, SIDE, FOLD, LANES), BF16),
            vmem((TEAM, SIDE, rows, LANES), BF16),
            vmem((TEAM, SIDE, SIDE * FOLD, LANES), BF16),
            vmem((TEAM, SLOTS, block, LANES), BF16),
            vmem((LANES, columns), BF16),
            vmem((block, columns), F32),
            vmem((block, columns), F32),
            vmem((SIZE + 8, columns), F32),
            vmem((8, columns), F32),
            vmem((TEAM, SIDE, SIDE * FOLD, LANES), BF16),
            vmem((TEAM, SIDE - 1, SIDE * FOLD, LANES), BF16),
            vmem((TEAM, SIDE, 8, 640), F32),
            vmem((TEAM, SIDE - 1, 8, 640), F32),
            vmem((2, block, LANES), BF16),
            vmem((2, SIDE, rows, LANES), BF16),
            dma((7,)), dma((6,)), dma((6,)), dma((2, 3)), dma((2, 3)), dma((2,)), dma((2,)),
            dma((6, 3)), dma((6, 3)), dma((TEAM, 3)), dma((TEAM, 3)),
            dma((TEAM, 3)), dma((TEAM, SLOTS)), dma((TEAM, SLOTS)),
            dma((TEAM, 6)), dma((TEAM, 6)), dma((2, 3)), dma((2, 3)),
        ],
        compiler_params=pltpu.CompilerParams(
            collective_id=0, has_side_effects=True, vmem_limit_bytes=56 * 2**20
        ),
        name="layer",
    )(tile_embeds, w_in, perturb, gain_attn, w_qkv, temper, w_out, gain_mlp, w_up, w_down)


def solution(mesh):
    placed = (P("grp", "seq"), P("grp", None), P("grp", None), P(), P(), P(), P(), P(), P(), P())
    return jax.shard_map(
        on_device, mesh=mesh, in_specs=placed, out_specs=P(("seq", "grp"), None), check_vma=False
    )
```

time: 103 us -> 94.4 us (0.917)
  Pallas kernels: 101 us -> 92.6 us
    pallas_call x1, Pallas kernels: 101 us -> 92.6 us  [on_device(): pl.pallas_call(layer_kernel, out_shape=jax.ShapeDtypeStruct((rows, width)...]
where the time goes in v2:
time: 94.4 us; the launch traced here: 94.2 us
  Pallas kernels  92.6 us (98%)
  local copies, waits for them, and re-layouts  1.64 us (2%)
    pallas_call x1, Pallas kernels, on_device(): pl.pallas_call(layer_kernel, out_shape=jax.ShapeDtypeStruct((rows, width)...  92.6 us

profile of v2, /device:TPU:0, one launch (start us, length us, event | category | flops | bytes accessed | tf_op | source)
XLA Modules:
  0.0 94.2 jit_solution(12657951245116949528)
XLA Ops:
  0.0 92.6 %layer.1 = bf16[144,768]{1,0:T(8,128)(2,1)} custom-call(bf16[192,1152]{1,0:T(8,128)(2,1)} %embeds_hbm.1, bf16[192,768]{1,0:T(8,128)(2,1)} %w_in_hbm.1, bf16[192,768]{1,0:T(8,128)(2,1)} %perturb_hbm.1, f32[768]{0:T(1024)} %gain_attn.1, bf16[768,2304]{1,0:T(8,128)(2,1)} %w_qkv_hbm.1, f32[12]{0:T(128)} %temper.1, bf16[768,768]{1,0:T(8,128)(2,1)} %w_out_hbm.1, ...), custom_call_target="tpu_custom_call" | custom-call | tf_op jit(solution)/shard_map/layer/pallas_call | solution.py:434
  92.6 1.6 %copy.12 = bf16[144,768]{1,0:T(8,128)(2,1)} copy(bf16[144,768]{1,0:T(8,128)(2,1)} %layer.1) | data formatting | bytes 442368

commit v3 on v2

--- a/solution.py
+++ b/solution.py
@@ -90,7 +90,7 @@
             (w_out_hbm, w_out), (w_up_hbm, w_up), (w_down_hbm, w_down),
         ])
     ]
-    for load in loads:
+    for load in loads[:3]:
         load.start()
     barrier = pltpu.get_barrier_semaphore()
     greeted = [to[d] for to in (x_to, y_to, z_to) for d in ahead] + [sibling]
@@ -111,10 +111,13 @@
     for side in range(2):
         w_all[0, side] = w_eff[:, side * half : (side + 1) * half]
     pl.semaphore_wait(barrier, len(greeted))
-    w_z, w_c = {}, {}
+    w_z, w_y, w_c = {}, {}, {}
+    quarter = w_in.shape[0] // SIDE
+    piece = pl.ds(pl.multiple_of(y * quarter, 16), quarter)
     for d in (1, 3, 2):
         w_z[d] = send(
-            w_all.at[0, core], w_all.at[d, core], w_send.at[d - 1], w_recv.at[d - 1], z_to[d]
+            w_all.at[0, core, piece], w_all.at[d, core, piece],
+            w_send.at[0, d - 1], w_recv.at[0, d - 1], z_to[d],
         )
     loads[0].wait()
     pair = 2 * rows
@@ -139,9 +142,19 @@
             )
     for d in (1, 3, 2):
         w_z[d].wait_recv()
+        for e in (1, 3, 2):
+            w_y[d, e] = send(
+                w_all.at[d, core, piece], w_all.at[d, core, piece],
+                w_send.at[e, d - 1], w_recv.at[e, d - 1], y_to[e],
+            )
+    for d in (1, 3, 2):
+        for e in (1, 3, 2):
+            w_y[d, e].wait_recv()
         w_c[d] = send(
-            w_all.at[d, core], w_all.at[d, core], w_send.at[d + 2], w_recv.at[d + 2], sibling
+            w_all.at[d, core], w_all.at[d, core], w_send.at[4, d - 1], w_recv.at[4, d - 1], sibling
         )
+    for load in loads[3:]:
+        load.start()
     lane = lax.broadcasted_iota(jnp.int32, (rows, LANES), 1)
 
     def part_sum(late, side):
@@ -211,16 +224,6 @@
             )
         q_all[head, 0, 0:FOLD] = q_out[head, y]
 
-    query = jnp.dot(normed, w_qkv[:, :width], preferred_element_type=F32)
-    exchange_q(0)
-    keys = jnp.dot(normed, w_qkv[:, width : 2 * width], preferred_element_type=F32)
-    values = jnp.dot(normed, w_qkv[:, 2 * width :], preferred_element_type=F32)
-    exchange_kv(0)
-    exchange_kv(1)
-    exchange_q(1)
-    exchange_kv(2)
-    exchange_q(2)
-
     kv_z = {}
     kv_c = {}
     q_x = {}
@@ -253,8 +256,17 @@
                 x_recv.at[head, d - 1], x_to[d],
             )
 
+    query = jnp.dot(normed, w_qkv[:, :width], preferred_element_type=F32)
+    exchange_q(0)
+    keys = jnp.dot(normed, w_qkv[:, width : 2 * width], preferred_element_type=F32)
+    values = jnp.dot(normed, w_qkv[:, 2 * width :], preferred_element_type=F32)
+    exchange_kv(0)
     spread_q(0)
+    exchange_kv(1)
+    exchange_q(1)
     spread_kv(0)
+    exchange_kv(2)
+    exchange_q(2)
     spread_kv(1)
     spread_q(1)
     spread_kv(2)
@@ -460,7 +472,7 @@
             vmem((TEAM, SIDE - 1, 8, 640), F32),
             vmem((2, block, LANES), BF16),
             vmem((2, SIDE, rows, LANES), BF16),
-            dma((7,)), dma((6,)), dma((6,)), dma((2, 3)), dma((2, 3)), dma((2,)), dma((2,)),
+            dma((7,)), dma((5, 3)), dma((5, 3)), dma((2, 3)), dma((2, 3)), dma((2,)), dma((2,)),
             dma((6, 3)), dma((6, 3)), dma((TEAM, 3)), dma((TEAM, 3)),
             dma((TEAM, 3)), dma((TEAM, SLOTS)), dma((TEAM, SLOTS)),
             dma((TEAM, 6)), dma((TEAM, 6)), dma((2, 3)), dma((2, 3)),

time: 94.4 us -> 92.3 us (0.978)
  Pallas kernels: 92.6 us -> 90.5 us
    pallas_call x1, Pallas kernels: 92.6 us -> 90.5 us  [on_device(): pl.pallas_call(layer_kernel, out_shape=jax.ShapeDtypeStruct((rows, width)...]
where the time goes in v3:
time: 92.3 us; the launch traced here: 92.1 us
  Pallas kernels  90.5 us (98%)
  local copies, waits for them, and re-layouts  1.64 us (2%)
    pallas_call x1, Pallas kernels, on_device(): pl.pallas_call(layer_kernel, out_shape=jax.ShapeDtypeStruct((rows, width)...  90.5 us

profile of v3, /device:TPU:0, one launch (start us, length us, event | category | flops | bytes accessed | tf_op | source)
XLA Modules:
  0.0 92.1 jit_solution(2563786843224956706)
XLA Ops:
  0.0 90.5 %layer.1 = bf16[144,768]{1,0:T(8,128)(2,1)} custom-call(bf16[192,1152]{1,0:T(8,128)(2,1)} %embeds_hbm.1, bf16[192,768]{1,0:T(8,128)(2,1)} %w_in_hbm.1, bf16[192,768]{1,0:T(8,128)(2,1)} %perturb_hbm.1, f32[768]{0:T(1024)} %gain_attn.1, bf16[768,2304]{1,0:T(8,128)(2,1)} %w_qkv_hbm.1, f32[12]{0:T(128)} %temper.1, bf16[768,768]{1,0:T(8,128)(2,1)} %w_out_hbm.1, ...), custom_call_target="tpu_custom_call" | custom-call | tf_op jit(solution)/shard_map/layer/pallas_call | solution.py:446
  90.5 1.6 %copy.12 = bf16[144,768]{1,0:T(8,128)(2,1)} copy(bf16[144,768]{1,0:T(8,128)(2,1)} %layer.1) | data formatting | bytes 442368

commit v4 on v3

--- a/solution.py
+++ b/solution.py
@@ -272,25 +272,33 @@
     spread_kv(2)
     spread_q(2)
 
-    columns = turned.shape[1]
+    columns = turned.shape[2]
     ones = jnp.ones((8, block), BF16)
     o_x, l_x = {}, {}
-    for head in range(TEAM):
+    strips = [slice(at, at + STRIP) for at in range(0, columns, STRIP)]
+
+    def await_queries(head):
         for d in ahead:
             q_x[head, d].wait_recv()
+
+    def turn_queries(head):
         for slot in range(SIDE):
             part = unfold(q_all.at[head, slot], rows)
             part = jnp.concatenate([part, jnp.zeros((block, LANES - SIZE), BF16)], axis=1)
-            turned[:, slot * block : (slot + 1) * block] = part.T
+            turned[head % 2, :, slot * block : (slot + 1) * block] = part.T
+
+    def score(head, slot, into, strip):
+        into[:, strip] = jnp.dot(
+            kv_all[head, slot], turned[head % 2, :, strip], preferred_element_type=F32
+        )
+
+    await_queries(0)
+    turn_queries(0)
+    for strip in strips:
+        score(0, 0, score_a, strip)
+    for head in range(TEAM):
         acc[...] = jnp.zeros(acc.shape, F32)
         peak[...] = jnp.full(peak.shape, -1e30, F32)
-
-        strips = [slice(at, at + STRIP) for at in range(0, columns, STRIP)]
-
-        def score(slot, into, strip, head=head):
-            into[:, strip] = jnp.dot(
-                kv_all[head, slot], turned[:, strip], preferred_element_type=F32
-            )
 
         def absorb(values, scores_ref, strip):
             scores = scores_ref[:, strip]
@@ -305,16 +313,14 @@
         def step_over(slot, now, later, into, head=head):
             values = jnp.concatenate([kv_all[head, slot].T[SIZE:], ones], axis=0)
             for strip in strips:
-                score(later, into, strip)
+                if later is not None:
+                    score(*later, into, strip)
                 absorb(values, now, strip)
 
         def wait_slot(slot, head=head):
             pltpu.make_async_copy(
                 kv_all.at[head, slot], kv_all.at[head, slot], kv_recv.at[head, slot]
             ).wait()
-
-        for strip in strips:
-            score(0, score_a, strip)
 
         def pair(step, _, head=head):
             @pl.when(step == 0)
@@ -335,21 +341,24 @@
                 forward_kv(head, 6)
                 wait_slot(5)
 
-            @pl.when(step == 3)
-            def _():
-                wait_slot(7)
-
-            step_over(2 * step, score_a, 2 * step + 1, score_b)
-            step_over(2 * step + 1, score_b, jnp.minimum(2 * step + 2, SLOTS - 1), score_a)
+            step_over(2 * step, score_a, (head, 2 * step + 1), score_b)
+            step_over(2 * step + 1, score_b, (head, 2 * step + 2), score_a)
             return 0
 
-        lax.fori_loop(0, SLOTS // 2, pair, 0)
+        lax.fori_loop(0, SLOTS // 2 - 1, pair, 0)
+        wait_slot(SLOTS - 1)
+        follows = head + 1 < TEAM
+        if follows:
+            await_queries(head + 1)
+        step_over(SLOTS - 2, score_a, (head, SLOTS - 1), score_b)
+        if follows:
+            turn_queries(head + 1)
+        step_over(SLOTS - 1, score_b, (head + 1, 0) if follows else None, score_a)
 
         sums_row = acc[SIZE : SIZE + 1, :]
         log_sum = peak[0:1, :] + jnp.log2(sums_row)
-        whole = jnp.concatenate(
-            [acc[0:SIZE, :] * (1.0 / sums_row), jnp.zeros((LANES - SIZE, columns), F32)], axis=0
-        )
+        whole = (acc[0:SIZE, :] * (1.0 / sums_row)).astype(BF16)
+        whole = jnp.concatenate([whole, jnp.zeros((LANES - SIZE, columns), BF16)], axis=0)
         for slot in (1, 3, 2, 0):
             area = slice(slot * block, (slot + 1) * block)
             upright = whole[:, area].T[:, :SIZE]
@@ -461,7 +470,7 @@
             vmem((TEAM, SIDE, rows, LANES), BF16),
             vmem((TEAM, SIDE, SIDE * FOLD, LANES), BF16),
             vmem((TEAM, SLOTS, block, LANES), BF16),
-            vmem((LANES, columns), BF16),
+            vmem((2, LANES, columns), BF16),
             vmem((block, columns), F32),
             vmem((block, columns), F32),
             vmem((SIZE + 8, columns), F32),

time: 92.3 us -> 88.5 us (0.959)
  Pallas kernels: 90.5 us -> 86.6 us
    pallas_call x1, Pallas kernels: 90.5 us -> 86.6 us  [on_device(): pl.pallas_call(layer_kernel, out_shape=jax.ShapeDtypeStruct((rows, width)...]
where the time goes in v4:
time: 88.5 us; the launch traced here: 88.3 us
  Pallas kernels  86.6 us (98%)
  local copies, waits for them, and re-layouts  1.64 us (2%)
    pallas_call x1, Pallas kernels, on_device(): pl.pallas_call(layer_kernel, out_shape=jax.ShapeDtypeStruct((rows, width)...  86.6 us

profile of v4, /device:TPU:0, one launch (start us, length us, event | category | flops | bytes accessed | tf_op | source)
XLA Modules:
  0.0 88.3 jit_solution(12730495208889716188)
XLA Ops:
  0.0 86.6 %layer.1 = bf16[144,768]{1,0:T(8,128)(2,1)} custom-call(bf16[192,1152]{1,0:T(8,128)(2,1)} %embeds_hbm.1, bf16[192,768]{1,0:T(8,128)(2,1)} %w_in_hbm.1, bf16[192,768]{1,0:T(8,128)(2,1)} %perturb_hbm.1, f32[768]{0:T(1024)} %gain_attn.1, bf16[768,2304]{1,0:T(8,128)(2,1)} %w_qkv_hbm.1, f32[12]{0:T(128)} %temper.1, bf16[768,768]{1,0:T(8,128)(2,1)} %w_out_hbm.1, ...), custom_call_target="tpu_custom_call" | custom-call | tf_op jit(solution)/shard_map/layer/pallas_call | solution.py:455
  86.6 1.6 %copy.12 = bf16[144,768]{1,0:T(8,128)(2,1)} copy(bf16[144,768]{1,0:T(8,128)(2,1)} %layer.1) | data formatting | bytes 442368
